TPU v7x, 512 devices: a whole 4x4x16 slice. The times are simulated.
512 devices in a mesh: ens: 8 (over z_hi, core), space: 64 (over z_lo, y, x).
Axes of the slice: x: 4, y: 4, z: 16 (z_hi: 4, z_lo: 4; z = z_hi * 4 + z_lo), core: 2. Of those that a mesh axis runs over, the one named last changes fastest.
Arguments:
- latents: bfloat16 [16, 8192, 1024], P('ens', 'space'), may hold values from -16 to 16
- queries: bfloat16 [16, 8192, 1024], P('ens', 'space'), may hold values from -192 to 192
- attn_keys: bfloat16 [16, 8192, 1024], P('ens', 'space'), may hold values from -6 to 6
- value_weight: bfloat16 [1024, 1024], P('space'), may hold values from -0.1875 to 0.1875
- decoder: bfloat16 [1024, 100], replicated, may hold values from -0.1875 to 0.1875
- targets: float32 [100, 8192], P(None, 'space'), may hold values from -8 to 8
- send_rows: int32 [2, 2048], P(None, 'space'), may hold values from 0 to 127, as said below
- neighbours: int32 [8192, 16], P('space'), may hold values from 0 to 191, as said below
- live_slots: int32 [8192], P('space'), may hold values from 8 to 16, as said below
- loss_multiplier: float32 [1], replicated, may hold values from 1 to 4
Outputs:
- loss_value: float32 [1], replicated
- grad_latents: bfloat16 [16, 8192, 1024], P('ens', 'space')
- grad_queries: bfloat16 [16, 8192, 1024], P('ens', 'space')
- grad_keys: bfloat16 [16, 8192, 1024], P('ens', 'space')
- grad_weight: float32 [1024, 1024], P('space')
Inputs may be any that keep to these rules, and one draw needn't show every extreme that they name: `send_rows`: row 0 of a shard's block lists 32 of its own rows, from the first half of the shard, read by the shard before it along space (wrapping); row 1 lists 32 rows from the second half, read by the shard after it. Repeats may occur. `neighbours`: entry [n, t] indexes the wide rows of n's shard: the 32 rows received from the shard before it in the order of its list, the shard's own 128 rows, then the 32 rows received from the shard after it. Slot 0 is the node itself. Repeats may occur and then count twice. Node n uses its first live_slots[n] slots.
All inputs are finite; a program needn't handle non-finite values.
Results may differ from a plain program's by a relative error of at most 0.015.
Values may be sent and summed in bfloat16 or wider, within the bound.
A program may use at most 128 MiB of HBM per device.

v0:
```python
import jax
import jax.numpy as jnp
from jax import lax
from jax.sharding import PartitionSpec as P

HEADS = 16


smooth = 0.1


def passed_along(block, axis, distance):
    devices = range(lax.axis_size(axis))
    route = [((i - distance) % len(devices), i) for i in devices]
    return lax.ppermute(block, axis, route)


def linkage(neighbour_ids, live_count, extent):
    slot_ids = jnp.arange(neighbour_ids.shape[1], dtype=jnp.int32)
    in_use = (slot_ids[None, :] < live_count[:, None]).astype(jnp.float32)
    target_ids = jnp.arange(extent, dtype=jnp.int32)
    matches = (neighbour_ids[:, :, None] == target_ids[None, None, :]).astype(jnp.float32)
    return jnp.sum(in_use[:, :, None] * matches, axis=1)


def attend_member(value_inputs, key_rows, query_rows, latent_rows, linkage_map, decoder):
    row_count, width = query_rows.shape
    extent = key_rows.shape[0]
    head_size = width // HEADS
    query_half = query_rows.astype(jnp.bfloat16).reshape(row_count, HEADS, head_size)
    key_half = key_rows.astype(jnp.bfloat16).reshape(extent, HEADS, head_size)
    value_half = value_inputs.astype(jnp.bfloat16).reshape(extent, HEADS, head_size)
    scores = jnp.einsum(
        "rhc,jhc->hrj", query_half, key_half, preferred_element_type=jnp.float32
    ) * head_size ** (-0.5)
    masked = jnp.where(linkage_map[None] > 0, scores, -1e30)
    largest = jnp.max(masked, axis=-1, keepdims=True)
    raised = linkage_map[None] * jnp.exp(masked - largest)
    attn_weight = (raised / jnp.sum(raised, axis=-1, keepdims=True)).astype(jnp.bfloat16)
    mixed = jnp.einsum(
        "hrj,jhc->rhc", attn_weight, value_half, preferred_element_type=jnp.float32
    ).reshape(row_count, width)
    output_rows = (latent_rows + mixed).astype(jnp.bfloat16)
    return jnp.einsum("rd,dc->cr", output_rows, decoder, preferred_element_type=jnp.float32)


def score_parts(prediction, observation, weighting):
    ensemble_members = prediction.shape[0]
    member_shift = prediction - observation[None]
    spread = jnp.sqrt(member_shift * member_shift + smooth * smooth)
    pair_total = jnp.zeros(observation.shape, jnp.float32)
    pairwise_slope = jnp.zeros(prediction.shape, jnp.float32)
    for member_index in range(ensemble_members):
        pairwise_distance = prediction - prediction[member_index][None]
        radius = jnp.sqrt(pairwise_distance * pairwise_distance + smooth * smooth)
        pair_total = pair_total + jnp.sum(radius - smooth, axis=0)
        pairwise_slope = pairwise_slope + pairwise_distance / radius
    score_terms = jnp.mean(spread - smooth, axis=0) - pair_total / (
        2.0 * ensemble_members * (ensemble_members - 1)
    )
    score_slope = weighting * (
        member_shift / spread / ensemble_members
        - pairwise_slope / (ensemble_members * (ensemble_members - 1))
    )
    return (score_slope, score_terms)


def body(
    latents,
    queries,
    attn_keys,
    value_weight,
    decoder,
    targets,
    send_rows,
    neighbours,
    live_slots,
    loss_multiplier,
):
    members, row_count, width = latents.shape
    halo_rows = send_rows.shape[1]
    extent = row_count + 2 * halo_rows
    space_size = lax.axis_size("space")
    leftward = send_rows[0]
    rightward = send_rows[1]
    from_left = passed_along(
        (jnp.take(latents, rightward, axis=1), jnp.take(attn_keys, rightward, axis=1)), "space", 1
    )
    from_right = passed_along(
        (jnp.take(latents, leftward, axis=1), jnp.take(attn_keys, leftward, axis=1)), "space", -1
    )
    wide_latents = jnp.concatenate([from_left[0], latents, from_right[0]], axis=1)
    broad_keys = jnp.concatenate([from_left[1], attn_keys, from_right[1]], axis=1)
    linkage_map = linkage(neighbours, live_slots, extent)
    whole_weight = lax.all_gather(value_weight, "space", axis=0, tiled=True)
    value_inputs = jnp.einsum(
        "mjd,de->mje", wide_latents, whole_weight, preferred_element_type=jnp.float32
    )

    def member_forward(bundle):
        member_values, member_keys, member_queries, member_latents = bundle
        return attend_member(
            member_values,
            member_keys.astype(jnp.float32),
            member_queries.astype(jnp.float32),
            member_latents.astype(jnp.float32),
            linkage_map,
            decoder,
        )

    prediction = lax.map(member_forward, (value_inputs, broad_keys, queries, latents))
    weighting = loss_multiplier[0]
    node_total = row_count * space_size * decoder.shape[1]
    every_member = lax.all_gather(prediction, "ens", axis=0, tiled=True)
    score_slope, score_terms = score_parts(every_member, targets, weighting)
    own_slope = lax.dynamic_slice_in_dim(score_slope, lax.axis_index("ens") * members, members, 0)
    loss_total = lax.psum(jnp.sum(score_terms), "space")
    loss_value = (loss_total / node_total).reshape(1)

    def backward_member(bundle):
        member_values, member_keys, member_queries, member_latents, member_slope = bundle

        def local_forward(value_in, key_in, query_in, latent_in):
            return attend_member(value_in, key_in, query_in, latent_in, linkage_map, decoder)

        unused, pullback = jax.vjp(
            local_forward,
            member_values,
            member_keys.astype(jnp.float32),
            member_queries.astype(jnp.float32),
            member_latents.astype(jnp.float32),
        )
        return pullback(member_slope)

    grad_values, grad_wkeys, grad_query, grad_resid = lax.map(
        backward_member, (value_inputs, broad_keys, queries, latents, own_slope)
    )
    value_grad_half = grad_values.astype(jnp.bfloat16)
    grad_wide = jnp.einsum(
        "mje,de->mjd", value_grad_half, whole_weight, preferred_element_type=jnp.float32
    )
    partial_weight = lax.psum_scatter(
        jnp.einsum(
            "mjd,mje->de", wide_latents, value_grad_half, preferred_element_type=jnp.float32
        ),
        "space",
        scatter_dimension=0,
        tiled=True,
    )
    grad_weight = lax.psum(partial_weight, "ens")
    upper_start = halo_rows + row_count
    back_from_right = passed_along(
        (grad_wide[:, :halo_rows], grad_wkeys[:, :halo_rows]), "space", -1
    )
    back_from_left = passed_along(
        (grad_wide[:, upper_start:], grad_wkeys[:, upper_start:]), "space", 1
    )
    latent_grad = grad_resid + grad_wide[:, halo_rows:upper_start]
    latent_grad = (
        latent_grad.at[:, rightward].add(back_from_right[0]).at[:, leftward].add(back_from_left[0])
    )
    key_grad = grad_wkeys[:, halo_rows:upper_start]
    key_grad = (
        key_grad.at[:, rightward].add(back_from_right[1]).at[:, leftward].add(back_from_left[1])
    )
    return (
        loss_value,
        latent_grad.astype(jnp.bfloat16),
        grad_query.astype(jnp.bfloat16),
        key_grad.astype(jnp.bfloat16),
        grad_weight,
    )


def solution(mesh):
    in_specs = (
        P("ens", "space", None),
        P("ens", "space", None),
        P("ens", "space", None),
        P("space", None),
        P(),
        P(None, "space"),
        P(None, "space"),
        P("space", None),
        P("space"),
        P(),
    )
    out_specs = (
        P(),
        P("ens", "space", None),
        P("ens", "space", None),
        P("ens", "space", None),
        P("space", None),
    )
    return jax.shard_map(body, mesh=mesh, in_specs=in_specs, out_specs=out_specs, check_vma=False)
```

profile of v0, /device:TPU:2, one launch (start us, length us, event | category | flops | bytes accessed | tf_op | source)
XLA Modules:
  0.0 1043.6 jit_solution(9493169386334166834)
XLA Ops:
  11.6 3.4 collective-permute-start
  17.1 6.4 collective-permute-start.1
  23.4 9.9 collective-permute-start.3
  43.6 325.1 %all-gather.2.cloned.1.call-done = bf16[1024,1024]{1,0:T(8,128)(2,1)} async-done(((bf16[16,1024]{1,0:T(8,128)(2,1)}), bf16[1024,1024]{1,0:T(8,128)(2,1)}) %all-gather.2.cloned.1.call-update) | async-done | bytes 2097168 | tf_op jit(solution)/shard_map/all_gather | solution.py:95
  368.7 3.1 fusion.38
  371.8 20.7 %while.26 = (s32[]{:T(128)}, f32[2,100,128]{2,1,0:T(8,128)}, bf16[2,128,1024]{2,1,0:T(8,128)(2,1)S(1)}, bf16[2,192,1024]{1,2,0:T(8,128)(2,1)S(1)}, f32[128,192]{...) while((s32[]{:T(128)}, f32[2,100,128]{2,1,0:T(8,128)}, ...), condition=%wide.region_4.6_spmd, body=%wide.region_1.5_spmd.sunk | while | flops 130048192 | bytes 9695349 | solution.py:111
  374.4 3.0 fusion.101
  377.5 2.6 fusion.102
  384.8 3.0 fusion.101
  387.8 2.6 fusion.102
  392.6 21.9 %all_gather.7 = f32[16,100,128]{2,1,0:T(8,128)S(1)} all-gather(f32[2,100,128]{2,1,0:T(8,128)} %get-tuple-element.108), channel_id=1, replica_groups=mesh['ens'=8,'space'=64] {'ens'}, dimensions={0}, use_global_device_ids=true | all-gather | bytes 921600 | tf_op jit(solution)/shard_map/all_gather | solution.py:114
  414.5 8.5 add_reduce_fusion.14
  424.5 21.7 %while.27 = (s32[]{:T(128)}, bf16[2,192,1024]{1,2,0:T(8,128)(2,1)}, f32[2,192,1024]{1,2,0:T(8,128)}, bf16[2,128,1024]{2,1,0:T(8,128)(2,1)}, f32[2,128,1024]{2,1,...) while((s32[]{:T(128)}, bf16[2,192,1024]{1,2,0:T(8,128)(2,1)}, ...), condition=%wide.region_30.32_spmd, body=%wide.region_24.31_spmd.sunk | while | flops 297230336 | bytes 47000832 | solution.py:135
  446.2 4.7 convolution_bitcast_fusion.1
  451.6 3.4 fusion.36
  456.0 3.7 collective-permute-start.4
  459.7 2.1 collective-permute-start.5
  463.6 2.1 fusion.54
  465.7 8.1 collective-permute-start.6
  477.4 348.4 %reduce-scatter.2.cloned.1.call-done = f32[16,1024]{1,0:T(8,128)} async-done(((f32[1024,1024]{1,0:T(8,128)}), f32[16,1024]{1,0:T(8,128)}) %reduce-scatter.2.cloned.1.call-update) | async-done | bytes 65552 | tf_op jit(solution)/shard_map/reduce_scatter | solution.py:142
  827.6 188.7 %psum.14 = f32[]{:T(128)} all-reduce(f32[]{:T(128)} %subtract_reduce_fusion), channel_id=1, replica_groups=mesh['ens'=8,'space'=64] {'space'}, use_global_device_ids=true, to_apply=%region_23.25 | all-reduce | flops 1 | bytes 8 | tf_op jit(solution)/shard_map/psum | solution.py:117
  1016.3 2.3 copy.96
  1022.3 2.0 scatter_fusion
  1029.1 2.0 scatter_fusion.2
  (182 shorter events, 69.3 us)
Async XLA Ops:
  7.2 361.5 %all-gather.2.cloned.1.call-start = ((), (), s32[]{:S(2)}) async-start(), calls=%async_computation.1 | async-start | bytes 2129920 | tf_op jit(solution)/shard_map/all_gather | solution.py:95
  7.9 817.9 %reduce-scatter.2.cloned.1.call-start = ((), (), s32[]{:S(2)}) async-start(), calls=%async_computation.2 | async-start | bytes 4259840 | tf_op jit(solution)/shard_map/reduce_scatter | solution.py:142
  11.6 23.7 %copy-start.26 = (s32[128]{0:T(128)S(1)}, s32[128]{0:T(128)}, u32[]{:S(2)}) copy-start(s32[128]{0:T(128)} %param.24) | copy-start | bytes 1540
  11.6 23.8 %copy-start.24 = (s32[128,16]{0,1:T(8,128)S(1)}, s32[128,16]{0,1:T(8,128)}, u32[]{:S(2)}) copy-start(s32[128,16]{0,1:T(8,128)} %param.23) | copy-start | bytes 24580
  11.6 25.9 %collective-permute-start = (bf16[2,32,1024]{2,1,0:T(8,128)(2,1)S(1)}, bf16[2,32,1024]{2,1,0:T(8,128)(2,1)S(1)}, u32[]{:S(2)}, u32[]{:S(2)}) collective-permute-start(bf16[2,32,1024]{2,1,0:T(8,128)(2,1)S(1)} %get-tuple-element.319), channel_id=1, source_target_pairs={{63,0},{0,1},{1,2},{2,3},{3,4},{4,5},{5,6},{6,7},{7,8},{8,9},{9,10... | collective-permute-start | bytes 393224 | tf_op jit(solution)/shard_map/ppermute | solution.py:15
  16.0 19.9 %copy-start.13 = (bf16[2,128,1024]{2,1,0:T(8,128)(2,1)S(1)}, bf16[2,128,1024]{2,1,0:T(8,128)(2,1)}, u32[]{:S(2)}) copy-start(bf16[2,128,1024]{2,1,0:T(8,128)(2,1)} %param.17) | copy-start | bytes 1572868
  17.1 24.3 %collective-permute-start.1 = (bf16[2,32,1024]{2,1,0:T(8,128)(2,1)S(1)}, bf16[2,32,1024]{2,1,0:T(8,128)(2,1)}, u32[]{:S(2)}, u32[]{:S(2)}) collective-permute-start(bf16[2,32,1024]{2,1,0:T(8,128)(2,1)S(1)} %get-tuple-element.321), channel_id=1, source_target_pairs={{1,0},{2,1},{3,2},{4,3},{5,4},{6,5},{7,6},{8,7},{9,8},{10,9},{11,1... | collective-permute-start | bytes 393224 | tf_op jit(solution)/shard_map/ppermute | solution.py:15
  23.4 14.8 %collective-permute-start.3 = (bf16[2,32,1024]{2,1,0:T(8,128)(2,1)S(1)}, bf16[2,32,1024]{2,1,0:T(8,128)(2,1)S(1)}, u32[]{:S(2)}, u32[]{:S(2)}) collective-permute-start(bf16[2,32,1024]{2,1,0:T(8,128)(2,1)S(1)} %get-tuple-element.320), channel_id=1, source_target_pairs={{1,0},{2,1},{3,2},{4,3},{5,4},{6,5},{7,6},{8,7},{9,8},{10,9},{11,1... | collective-permute-start | bytes 393224 | tf_op jit(solution)/shard_map/ppermute | solution.py:15
  33.4 6.9 collective-permute-start.2
  43.6 328.2 %copy-start.1 = (bf16[1024,100]{0,1:T(8,128)(2,1)S(1)}, bf16[1024,100]{0,1:T(8,128)(2,1)}, u32[]{:S(2)}) copy-start(bf16[1024,100]{0,1:T(8,128)(2,1)} %param.20) | copy-start | bytes 614404
  392.6 21.9 %copy-start.23 = (f32[100,128]{1,0:T(8,128)S(1)}, f32[100,128]{1,0:T(8,128)}, u32[]{:S(2)}) copy-start(f32[100,128]{1,0:T(8,128)} %param.21) | copy-start | bytes 153604
  450.9 583.5 %all-reduce.2.cloned.1.call-start = ((), (), s32[]{:S(2)}) async-start(), calls=%async_computation.3 | async-start | bytes 131072 | tf_op jit(solution)/shard_map/psum | solution.py:150
  456.0 564.0 %collective-permute-start.4 = (f32[2,32,1024]{2,1,0:T(8,128)}, f32[2,32,1024]{2,1,0:T(8,128)}, u32[]{:S(2)}, u32[]{:S(2)}) collective-permute-start(f32[2,32,1024]{2,1,0:T(8,128)} %get-tuple-element.289), channel_id=1, source_target_pairs={{1,0},{2,1},{3,2},{4,3},{5,4},{6,5},{7,6},{8,7},{9,8},{10,9},{11,1... | collective-permute-start | bytes 786440 | tf_op jit(solution)/shard_map/ppermute | solution.py:15
  459.7 561.5 %collective-permute-start.5 = (f32[2,32,1024]{2,1,0:T(8,128)}, f32[2,32,1024]{2,1,0:T(8,128)}, u32[]{:S(2)}, u32[]{:S(2)}) collective-permute-start(f32[2,32,1024]{2,1,0:T(8,128)} %get-tuple-element.288), channel_id=1, source_target_pairs={{63,0},{0,1},{1,2},{2,3},{3,4},{4,5},{5,6},{6,7},{7,8},{8,9},{9,10... | collective-permute-start | bytes 786440 | tf_op jit(solution)/shard_map/ppermute | solution.py:15
  461.8 13.9 %copy-start.11 = (f32[16,100,128]{2,1,0:T(8,128)S(1)}, f32[16,100,128]{2,1,0:T(8,128)}, u32[]{:S(2)}) copy-start(f32[16,100,128]{2,1,0:T(8,128)} %copy-done.10) | copy-start | bytes 2457604
  463.6 12.5 %copy-start.7 = (f32[16,100,128]{2,1,0:T(8,128)S(1)}, f32[16,100,128]{2,1,0:T(8,128)}, u32[]{:S(2)}) copy-start(f32[16,100,128]{2,1,0:T(8,128)} %copy-done.6) | copy-start | bytes 2457604
  463.6 12.5 %copy-start.9 = (f32[16,100,128]{2,1,0:T(8,128)S(1)}, f32[16,100,128]{2,1,0:T(8,128)}, u32[]{:S(2)}) copy-start(f32[16,100,128]{2,1,0:T(8,128)} %copy-done.8) | copy-start | bytes 2457604
  465.7 11.1 %copy-start.18 = (f32[100,128]{1,0:T(8,128)S(1)}, f32[100,128]{1,0:T(8,128)}, u32[]{:S(2)}) copy-start(f32[100,128]{1,0:T(8,128)} %get-tuple-element.218) | copy-start | bytes 153604
  465.7 11.1 %copy-start.19 = (f32[100,128]{1,0:T(8,128)S(1)}, f32[100,128]{1,0:T(8,128)}, u32[]{:S(2)}) copy-start(f32[100,128]{1,0:T(8,128)} %get-tuple-element.219) | copy-start | bytes 153604
  465.7 11.1 %copy-start.20 = (f32[100,128]{1,0:T(8,128)S(1)}, f32[100,128]{1,0:T(8,128)}, u32[]{:S(2)}) copy-start(f32[100,128]{1,0:T(8,128)} %get-tuple-element.220) | copy-start | bytes 153604
  465.7 11.1 %copy-start.21 = (f32[100,128]{1,0:T(8,128)S(1)}, f32[100,128]{1,0:T(8,128)}, u32[]{:S(2)}) copy-start(f32[100,128]{1,0:T(8,128)} %get-tuple-element.221) | copy-start | bytes 153604
  465.7 11.1 %copy-start.22 = (f32[100,128]{1,0:T(8,128)S(1)}, f32[100,128]{1,0:T(8,128)}, u32[]{:S(2)}) copy-start(f32[100,128]{1,0:T(8,128)} %get-tuple-element.222) | copy-start | bytes 153604
  465.7 562.0 %collective-permute-start.6 = (f32[2,32,1024]{2,1,0:T(8,128)}, f32[2,32,1024]{2,1,0:T(8,128)}, u32[]{:S(2)}, u32[]{:S(2)}) collective-permute-start(f32[2,32,1024]{2,1,0:T(8,128)} %get-tuple-element.287), channel_id=1, source_target_pairs={{1,0},{2,1},{3,2},{4,3},{5,4},{6,5},{7,6},{8,7},{9,8},{10,9},{11,1... | collective-permute-start | bytes 786440 | tf_op jit(solution)/shard_map/ppermute | solution.py:15
  473.8 555.1 %collective-permute-start.7 = (f32[2,32,1024]{2,1,0:T(8,128)}, f32[2,32,1024]{2,1,0:T(8,128)S(1)}, u32[]{:S(2)}, u32[]{:S(2)}) collective-permute-start(f32[2,32,1024]{2,1,0:T(8,128)} %get-tuple-element.286), channel_id=1, source_target_pairs={{63,0},{0,1},{1,2},{2,3},{3,4},{4,5},{5,6},{6,7},{7,8},{8,9},{9,10... | collective-permute-start | bytes 786440 | tf_op jit(solution)/shard_map/ppermute | solution.py:15
  (21 other events, 89.6 us)
Sparse Core Ops, SparseCore 0:
  10.1 358.5 all-gather.1
  451.1 374.7 reduce-scatter.1
  829.0 96.2 all-reduce.1
where the time goes:
time: 1040 us
  waiting for transfers between devices  676 us (65%)
  blocking collectives  211 us (20%)
  local copies, waits for them, and re-layouts  41.4 us (4%)
  starting transfers between devices  37.5 us (4%)
  matrix products  33.9 us (3%)
  other arithmetic  27.1 us (3%)
  between operations  16.8 us (2%)
    reduce_scatter x1, waiting for transfers between devices, body(): lax.psum_scatter(jnp.einsum('mjd,mje->de', wide_latents, value_grad_half,...  348 us
    all_gather x1, waiting for transfers between devices, body(): whole_weight = lax.all_gather(value_weight, 'space', axis=0, tiled=True)  325 us
    psum x1, blocking collectives, body(): loss_total = lax.psum(jnp.sum(score_terms), 'space')  189 us
    ppermute x8, starting transfers between devices, passed_along(): return lax.ppermute(block, axis, route)  37.4 us
    all_gather x1, blocking collectives, body(): every_member = lax.all_gather(prediction, 'ens', axis=0, tiled=True)  21.9 us
  transfers between devices with their start and end apart: 11, of which 3 were waited for; matrix products, arithmetic and copies ran while one was open for 4% of the time, Pallas kernels for 0%

commit v1 on v0

v1 whole, which is shorter than its diff:
```python
import jax
import jax.numpy as jnp
from jax import lax
from jax.experimental import pallas as pl
from jax.experimental.pallas import tpu as pltpu
from jax.sharding import PartitionSpec as P

MESH = pl.DeviceIdType.MESH
F32 = jnp.float32
BF16 = jnp.bfloat16
M, R, D, H, W = 2, 128, 1024, 32, 192
PAIRS = 8
CH = 13
MEMBERS = 16
CHANNELS = 100
SMOOTH = 0.1
NT = (((1,), (1,)), ((), ()))
TN = (((0,), (0,)), ((), ()))


def dot(a, b, dims=(((1,), (0,)), ((), ()))):
    return lax.dot_general(a, b, dims, preferred_element_type=F32)


def iota(shape, dim):
    return lax.broadcasted_iota(jnp.int32, shape, dim)


def kernel(
    L, Q, K, wsh, dec, tgt, srows, nbr, live, mult,
    o_loss, o_dl, o_dq, o_dk, o_dw,
    wg, wf, wl, kw, qt, lt, wlt, lk, oneh, snd_l, snd_k,
    decp, decpt, tgo, pf, pb, vv, outt, fs, fa, sl, sr, dot_t, dv, dk, rv, rk,
    e1s, e1r, s1, r1, a2, s2, r2, a3, s3, r3, s4, r4, fin, lsend, lrecv,
    ssem, rsem,
):
    e = lax.axis_index("ens")
    s = lax.axis_index("space")
    zh, c = e // 2, e % 2
    zl, y, x = s // 16, (s // 4) % 4, s % 4
    a = y * (1 - c) + x * c
    b = x * (1 - c) + y * c
    b_other = y * (1 - c) + x * c

    def at(e_, zl_, y_, x_):
        return (e_, zl_ * 16 + y_ * 4 + x_)

    sibling = (zh * 2 + 1 - c, s)

    def peer_a(k):
        return at(e, zl, (y + k * (1 - c)) % 4, (x + k * c) % 4)

    def peer_b(k):
        return at(e, zl, (y + k * c) % 4, (x + k * (1 - c)) % 4)

    def peer_zl(k):
        return at(e, (zl + k) % 4, y, x)

    def peer_zh(k):
        return (((zh + k) % 4) * 2 + c, s)

    def peer_ens(k):
        return ((e + k) % 8, s)

    right = (e, (s + 1) % 64)
    left = (e, (s + 63) % 64)

    barrier = pltpu.get_barrier_semaphore()
    partners = [peer_a(k) for k in (1, 2, 3)] + [peer_b(k) for k in (1, 2, 3)]
    partners += [peer_zl(k) for k in (1, 2, 3)] + [peer_ens(k) for k in range(1, 8)]
    partners += [right, left]
    for p in partners:
        pl.semaphore_signal(barrier, inc=1, device_id=p, device_id_type=MESH)

    sent = []
    count = [0]

    def send(src, dst, device):
        k = count[0]
        count[0] += 1
        copy = pltpu.make_async_remote_copy(
            src_ref=src, dst_ref=dst, send_sem=ssem.at[k], recv_sem=rsem.at[k],
            device_id=device, device_id_type=MESH,
        )
        copy.start()
        sent.append(copy)
        return copy

    rows = iota((R, H), 0)
    to_right = (rows == srows[1:2, :]).astype(F32).astype(BF16)
    to_left = (rows == srows[0:1, :]).astype(F32).astype(BF16)
    oneh[:, 0:H] = to_right
    oneh[:, H:2 * H] = to_left
    for m in range(M):
        snd_k[0, m] = dot(to_right, K[m], TN).astype(BF16)
        snd_k[1, m] = dot(to_left, K[m], TN).astype(BF16)
        snd_l[0, m] = dot(to_right, L[m], TN).astype(BF16)
        snd_l[1, m] = dot(to_left, L[m], TN).astype(BF16)
    wg[c, b, zl, a] = wsh[:, pl.ds(pl.multiple_of(c * 512, 512), 512)]

    pl.semaphore_wait(barrier, len(partners))

    w1 = [send(wg.at[c, b, zl, a], wg.at[c, b, zl, a], peer_zl(k)) for k in (1, 2, 3)]
    hk = [
        send(snd_k.at[0], kw.at[:, pl.ds(R, H)], right),
        send(snd_k.at[1], kw.at[:, pl.ds(R + H, H)], left),
    ]

    for m in range(M):
        wl[m, 0:R] = L[m]
        kw[m, 0:R] = K[m]
    node_ids = dot((iota((16, 16), 0) == iota((16, 16), 1)).astype(F32).astype(BF16),
                   nbr[...].astype(F32).astype(BF16), NT)
    row = iota((W, R), 0)
    wide_id = jnp.where(row < R, row + H, jnp.where(row < R + H, row - R, row)).astype(F32)
    used = live[...]
    links = jnp.zeros((W, R), F32)
    for t in range(16):
        hit = jnp.where(used > t, node_ids[t:t + 1, :], -1.0) == wide_id
        links = links + jnp.where(hit, 1.0, 0.0)
    lk[:, 0:R] = links
    lk[:, R:2 * R] = links

    for k in range(3):
        w1[k].wait_recv()
    w2 = [send(wg.at[c, b, :, a], wg.at[c, b, :, a], peer_a(k)) for k in (1, 2, 3)]
    hl = [
        send(snd_l.at[0], wl.at[:, pl.ds(R, H)], right),
        send(snd_l.at[1], wl.at[:, pl.ds(R + H, H)], left),
    ]

    for m in range(M):
        for d in range(8):
            qt[m, d * 128:(d + 1) * 128, :] = Q[m, :, d * 128:(d + 1) * 128].T
            lt[m, d * 128:(d + 1) * 128, :] = L[m, :, d * 128:(d + 1) * 128].T
    slot, chan = iota((128, CHANNELS), 0), iota((128, CHANNELS), 1)
    place = ((slot % 16 < CH) & (chan == (slot // 16) * CH + slot % 16)).astype(F32).astype(BF16)
    decp[...] = dot(dec[...], place, NT).astype(BF16)
    decpt[...] = dot(place, dec[...], NT).astype(BF16)
    slot16, chan16 = iota((16, CHANNELS), 0), iota((16, CHANNELS), 1)
    own_place = ((slot16 < CH) & (chan16 == e * CH + slot16)).astype(F32)
    tgo[...] = lax.dot_general(
        own_place, tgt[...], (((1,), (0,)), ((), ())),
        precision=lax.Precision.HIGHEST, preferred_element_type=F32,
    )

    for k in range(3):
        w2[k].wait_recv()
    w3 = [send(wg.at[c, b], wg.at[c, b], peer_b(k)) for k in (1, 2, 3)]
    wd = [send(wg.at[c, b], wg.at[c, b], sibling)]

    for k in range(2):
        hk[k].wait_recv()

    top = iota((128, R), 0) < 64

    def spread(block):
        zero = jnp.zeros_like(block)
        return jnp.concatenate([jnp.where(top, block, zero), jnp.where(top, zero, block)], axis=1)

    def folded(block):
        return jnp.where(top, block[:, 0:R], block[:, R:2 * R])

    def cols(p):
        return pl.ds(pl.multiple_of(p * 128, 128), 128)

    def weights_of(p, _):
        link = lk[...]
        for m in range(M):
            scores = dot(kw[m, :, cols(p)], spread(qt[m, cols(p), :])) * 0.125
            masked = jnp.where(link > 0, scores, -1e30)
            raised = link * jnp.exp(masked - jnp.max(masked, axis=0, keepdims=True))
            weight = raised * (1.0 / jnp.sum(raised, axis=0, keepdims=True))
            pf[m, p] = weight
            pb[m, p] = weight.astype(BF16)
        return 0

    lax.fori_loop(0, 4, weights_of, 0)
    for k in range(3):
        w3[k].wait_recv()
        bk = (b + 3 - k) % 4
        wd.append(send(wg.at[c, bk], wg.at[c, bk], sibling))
    lax.fori_loop(4, PAIRS, weights_of, 0)
    for k in range(2):
        hl[k].wait_recv()
    for k in range(4):
        wd[k].wait_recv()

    for z_ in range(4):
        for y_ in range(4):
            for x_ in range(4):
                d = z_ * 256 + y_ * 64 + x_ * 16
                wf[d:d + 16, 0:512] = wg[0, x_, z_, y_]
                wf[d:d + 16, 512:1024] = wg[1, y_, z_, x_]

    def mix(m):
        def step(p, _):
            mixed = folded(dot(vv[m, :, cols(p)], pb[m, p], TN))
            outt[m, cols(p), :] = (lt[m, cols(p), :].astype(F32) + mixed).astype(BF16)
            return 0
        return step

    def values_of(m):
        def step(q, _):
            block = pl.ds(pl.multiple_of(q * 256, 256), 256)
            vv[m, :, block] = dot(wl[m], wf[:, block]).astype(BF16)
            return 0
        return step

    fx = []
    for m in range(M):
        lax.fori_loop(0, 4, values_of(m), 0)
        lax.fori_loop(0, PAIRS, mix(m), 0)
        fs[m] = dot(decpt[...], outt[m]).reshape(8, 16, R)
        fa[2 * e + m] = fs[m, e]
        for k in range(1, 8):
            fx.append(send(fs.at[m, (e + k) % 8], fa.at[2 * e + m], peer_ens(k)))

    for m in range(M):
        for d in range(8):
            halo_t = wl[m, R:W, d * 128:(d + 1) * 128].T
            own_t = lt[m, d * 128:(d + 1) * 128, :]
            for i in range(8):
                g = d * 8 + i
                z_, y_, x_ = g // 16, (g // 4) % 4, g % 4
                r0 = (x_ * 16 + z_ * 4 + y_) * 16
                r1_ = (y_ * 16 + z_ * 4 + x_) * 16
                for h, r_ in ((0, r0), (1, r1_)):
                    wlt[h, m, r_:r_ + 16, 0:R] = own_t[i * 16:(i + 1) * 16]
                    wlt[h, m, r_:r_ + 16, R:W] = halo_t[i * 16:(i + 1) * 16]

    for copy in fx:
        copy.wait_recv()

    f = fa[...]
    shift = f - tgo[...][None]
    square = shift * shift + SMOOTH * SMOOTH
    inverse = lax.rsqrt(square)
    near = jnp.sum(square * inverse - SMOOTH, axis=0)
    pair_slope = jnp.zeros((MEMBERS, 16, R), F32)
    pair_total = jnp.zeros((16, R), F32)
    for k in range(1, 9):
        other = jnp.concatenate([f[k:], f[:k]], axis=0)
        gap = f - other
        sq = gap * gap + SMOOTH * SMOOTH
        inv = lax.rsqrt(sq)
        radius = sq * inv - SMOOTH
        slope = gap * inv
        if k < 8:
            pair_total = pair_total + jnp.sum(radius, axis=0)
            pair_slope = pair_slope + slope - jnp.concatenate([slope[MEMBERS - k:], slope[:MEMBERS - k]], axis=0)
        else:
            pair_total = pair_total + jnp.sum(radius[:8], axis=0)
            pair_slope = pair_slope + slope
    pair_norm = 1.0 / (MEMBERS * (MEMBERS - 1))
    sl[...] = (mult[0] * (shift * inverse * (1.0 / MEMBERS) - pair_slope * pair_norm)).astype(BF16)
    slot_id = iota((16, R), 0)
    real = (slot_id < CH) & (slot_id + e * CH < CHANNELS)
    terms = jnp.where(real, near * (1.0 / MEMBERS) - pair_total * pair_norm, 0.0)
    sr[e] = sl[pl.ds(2 * e, 2)]
    sx = [
        send(sl.at[pl.ds(2 * ((e + k) % 8), 2)], sr.at[e], peer_ens(k))
        for k in range(1, 8)
    ]
    lsend[0] = terms[0:8] + terms[8:16]
    l0 = send(lsend.at[0], lrecv.at[0, 0], sibling)
    for copy in sx:
        copy.wait_recv()

    for m in range(M):
        dot_t[m] = dot(decp[...], sr[:, m].reshape(128, R)).astype(BF16)

    def value_grads(half):
        def step(q, _):
            p = half * 4 + q
            for m in range(M):
                dv[half, m, :, cols(q)] = dot(pb[m, p], spread(dot_t[m, cols(p), :]), NT).astype(BF16)
            return 0
        lax.fori_loop(0, 4, step, 0)

    def weight_grad(half, block):
        block_rows = pl.ds(pl.multiple_of(block * 256, 256), 256)
        return dot(wlt[half, 0, block_rows, :], dv[half, 0]) + dot(wlt[half, 1, block_rows, :], dv[half, 1])

    value_grads(1 - c)
    x1 = []
    for k in (1, 2, 3, 0):
        block = (b_other + k) % 4
        e1s[k] = weight_grad(1 - c, block).astype(BF16)
        x1.append(send(e1s.at[k], e1r.at[k], sibling))
    value_grads(c)
    hv = [
        send(dv.at[:, :, pl.ds(R + H, H)], rv.at[:, :, pl.ds(H, H)], right),
        send(dv.at[:, :, pl.ds(R, H)], rv.at[:, :, pl.ds(0, H)], left),
    ]
    l0.wait_recv()
    lsend[1] = lsend[0] + lrecv[0, 0]
    lrecv[1, b] = lsend[1]
    x2 = []
    l1 = [send(lsend.at[1], lrecv.at[1, b], peer_b(k)) for k in (1, 2, 3)]
    for i, k in enumerate((1, 2, 3, 0)):
        total = weight_grad(c, (b + k) % 4)
        x1[i].wait_recv()
        total = total + e1r[k].astype(F32)
        if k:
            s1[k - 1] = total.astype(BF16)
            x2.append(send(s1.at[k - 1], r1.at[k - 1], peer_b(k)))
        else:
            a2[...] = total.reshape(4, 4, 16, 512)

    def attention_grads(p, _):
        for m in range(M):
            grad_weight = dot(vv[m, :, cols(p)], spread(dot_t[m, cols(p), :])).astype(BF16).astype(F32)
            weight = pf[m, p]
            drift = jnp.sum(grad_weight * weight, axis=0, keepdims=True)
            grad_scores = (weight * (grad_weight - drift) * 0.125).astype(BF16)
            dk[m, :, cols(p)] = dot(grad_scores, spread(qt[m, cols(p), :]), NT).astype(BF16)
            grad_q = folded(dot(kw[m, :, cols(p)], grad_scores, TN))
            o_dq[m, :, cols(p)] = grad_q.astype(BF16).T
        return 0

    lax.fori_loop(0, PAIRS, attention_grads, 0)
    hkb = [
        send(dk.at[:, pl.ds(R + H, H)], rk.at[:, pl.ds(H, H)], right),
        send(dk.at[:, pl.ds(R, H)], rk.at[:, pl.ds(0, H)], left),
    ]

    def loss_step(stage, copies, mine, peers):
        for copy in copies:
            copy.wait_recv()
        got = lrecv[stage]
        lsend[stage + 1] = (got[0] + got[1]) + (got[2] + got[3])
        if peers is None:
            return None
        lrecv[stage + 1, mine] = lsend[stage + 1]
        return [send(lsend.at[stage + 1], lrecv.at[stage + 1, mine], p) for p in peers]

    for k in range(3):
        x2[k].wait_recv()
    a2[...] = a2[...] + (
        r1[0].astype(F32) + r1[1].astype(F32) + r1[2].astype(F32)
    ).reshape(4, 4, 16, 512)
    x3 = []
    for k in (1, 2, 3):
        s2[k - 1] = a2[:, (a + k) % 4].astype(BF16)
        x3.append(send(s2.at[k - 1], r2.at[k - 1], peer_a(k)))
    l2 = loss_step(1, l1, a, [peer_a(k) for k in (1, 2, 3)])

    for copy in hv:
        copy.wait_recv()
    for m in range(M):
        parts = [
            (dv[h, m, 0:R].astype(F32) + dot(oneh[...], rv[h, m])).astype(BF16) for h in range(2)
        ]
        out = dot(sr[:, m].reshape(128, R), decpt[...], TN).astype(BF16).astype(F32)
        out = out + dot(parts[0], wf[:, 0:512], NT) + dot(parts[1], wf[:, 512:1024], NT)
        o_dl[m] = out.astype(BF16)

    for k in range(3):
        x3[k].wait_recv()
    a3[...] = a2[:, a] + (r2[0].astype(F32) + r2[1].astype(F32) + r2[2].astype(F32))
    x4 = []
    for k in (1, 2, 3):
        s3[k - 1] = a3[(zl + k) % 4].astype(BF16)
        x4.append(send(s3.at[k - 1], r3.at[k - 1], peer_zl(k)))
    l3 = loss_step(2, l2, zl, [peer_zl(k) for k in (1, 2, 3)])

    for copy in hkb:
        copy.wait_recv()
    for m in range(M):
        o_dk[m] = (dk[m, 0:R].astype(F32) + dot(oneh[...], rk[m])).astype(BF16)

    for k in range(3):
        x4[k].wait_recv()
    s4[...] = (a3[zl] + (r3[0].astype(F32) + r3[1].astype(F32) + r3[2].astype(F32))).astype(BF16)
    r4[zh] = s4[...]
    x5 = [send(s4, r4.at[zh], peer_zh(k)) for k in (1, 2, 3)]
    l4 = loss_step(3, l3, zh, [peer_zh(k) for k in (1, 2, 3)])
    for k in range(3):
        x5[k].wait_recv()
    fin[c] = (r4[0].astype(F32) + r4[1].astype(F32)) + (r4[2].astype(F32) + r4[3].astype(F32))
    x6 = send(fin.at[c], fin.at[c], sibling)
    loss_step(4, l4, None, None)
    lrecv[5, c] = lsend[5]
    l5 = send(lsend.at[5], lrecv.at[5, c], sibling)
    x6.wait_recv()
    o_dw[:, 0:512] = fin[0]
    o_dw[:, 512:1024] = fin[1]
    l5.wait_recv()
    o_loss[0, 0] = jnp.sum(lrecv[5, 0]) * (1.0 / (8192 * CHANNELS))
    for copy in sent:
        copy.wait_send()


N_COPIES = 96


def body(latents, queries, attn_keys, value_weight, decoder, targets, send_rows, neighbours, live_slots, loss_multiplier):
    vm = pl.BlockSpec(memory_space=pltpu.VMEM)
    sm = pl.BlockSpec(memory_space=pltpu.SMEM)

    def buf(*shape, dtype=BF16):
        return pltpu.VMEM(shape, dtype)

    scratch = [
        buf(2, 4, 4, 4, 16, 512),
        buf(D, D),
        buf(M, W, D),
        buf(M, W, D),
        buf(M, D, R),
        buf(M, D, R),
        buf(2, M, D, W),
        buf(W, 2 * R, dtype=F32),
        buf(R, 2 * H),
        buf(2, M, H, D),
        buf(2, M, H, D),
        buf(D, 128),
        buf(128, D),
        buf(16, R, dtype=F32),
        buf(M, PAIRS, W, 2 * R, dtype=F32),
        buf(M, PAIRS, W, 2 * R),
        buf(M, W, D),
        buf(M, D, R),
        buf(M, 8, 16, R, dtype=F32),
        buf(MEMBERS, 16, R, dtype=F32),
        buf(MEMBERS, 16, R),
        buf(8, M, 16, R),
        buf(M, D, R),
        buf(2, M, W, 512),
        buf(M, W, D),
        buf(2, M, 2 * H, 512),
        buf(M, 2 * H, D),
        buf(4, 256, 512),
        buf(4, 256, 512),
        buf(3, 256, 512),
        buf(3, 256, 512),
        buf(4, 4, 16, 512, dtype=F32),
        buf(3, 4, 16, 512),
        buf(3, 4, 16, 512),
        buf(4, 16, 512, dtype=F32),
        buf(3, 16, 512),
        buf(3, 16, 512),
        buf(16, 512),
        buf(4, 16, 512),
        buf(2, 16, 512, dtype=F32),
        buf(6, 8, 128, dtype=F32),
        buf(6, 4, 8, 128, dtype=F32),
        pltpu.SemaphoreType.DMA((N_COPIES,)),
        pltpu.SemaphoreType.DMA((N_COPIES,)),
    ]
    loss, dl, dq, dk, dw = pl.pallas_call(
        kernel,
        out_shape=(
            jax.ShapeDtypeStruct((1, 1), F32),
            jax.ShapeDtypeStruct((M, R, D), BF16),
            jax.ShapeDtypeStruct((M, R, D), BF16),
            jax.ShapeDtypeStruct((M, R, D), BF16),
            jax.ShapeDtypeStruct((16, D), F32),
        ),
        in_specs=[vm] * 9 + [sm],
        out_specs=(sm, vm, vm, vm, vm),
        scratch_shapes=scratch,
        compiler_params=pltpu.CompilerParams(
            collective_id=0, has_side_effects=True, vmem_limit_bytes=56 * 1024 * 1024
        ),
    )(
        latents, queries, attn_keys, value_weight, decoder, targets, send_rows, neighbours,
        live_slots.reshape(1, R), loss_multiplier,
    )
    return loss.reshape(1), dl, dq, dk, dw


def solution(mesh):
    rows = P("ens", "space", None)
    in_specs = (
        rows, rows, rows, P("space", None), P(), P(None, "space"), P(None, "space"),
        P("space", None), P("space"), P(),
    )
    out_specs = (P(), rows, rows, rows, P("space", None))
    return jax.shard_map(body, mesh=mesh, in_specs=in_specs, out_specs=out_specs, check_vma=False)
```

time: 1040 us -> 112 us (0.11)
  the two profiles are of different devices: /device:TPU:2 before, /device:TPU:1 now
where the time goes in v1:
time: 112 us
  Pallas kernels  101 us (90%)
  local copies, waits for them, and re-layouts  7.87 us (7%)
  between operations  3.06 us (3%)
    pallas_call x1, Pallas kernels, body(): pl.pallas_call(kernel, out_shape=(jax.ShapeDtypeStruct((1, 1), F32), jax....  101 us
    unnamed x12, local copies, waits for them, and re-layouts  7.87 us

profile of v1, /device:TPU:1, one launch (start us, length us, event | category | flops | bytes accessed | tf_op | source)
XLA Modules:
  0.0 111.9 jit_solution(6676680498970329623)
XLA Ops:
  1.3 1.4 %copy.16.nbr = s32[128,16]{1,0:T(8,128)} copy(s32[128,16]{0,1:T(8,128)} %param.17) | data formatting | bytes 16384 | tf_op args[7]
  2.7 1.8 %copy.15.dec = bf16[1024,100]{1,0:T(8,128)(2,1)} copy(bf16[1024,100]{0,1:T(8,128)(2,1)} %param.14) | data formatting | bytes 409600 | tf_op args[4]
  4.5 100.9 %shard_map.137 = (f32[1,1]{1,0:T(1,128)}, bf16[2,128,1024]{2,1,0:T(8,128)(2,1)}, bf16[2,128,1024]{2,1,0:T(8,128)(2,1)}, bf16[2,128,1024]{2,1,0:T(8,128)(2,1)}, f32[16,1024]{1,0:T(8,128)}) custom-call(bf16[2,128,1024]{2,1,0:T(8,128)(2,1)} %L.1, bf16[2,128,1024]{2,1,0:T(8,128)(2,1)} %Q.1, bf16[2,128,1024]{2,1,0:T(8,128)(2,1)} %K.1, bf16[16,1024]{1,0:T(8,128)(2,1)} %wsh.1, ...), custom_call_target="tpu_custom_call" | custom-call | tf_op jit(solution)/shard_map/pallas_call | solution.py:451
  106.1 0.0 copy-start.1
  106.1 1.9 %copy.24 = bf16[2,128,1024]{2,1,0:T(8,128)(2,1)} copy(bf16[2,128,1024]{2,1,0:T(8,128)(2,1)} %get-tuple-element.21) | data formatting | bytes 1048576
  108.0 0.0 copy-done.1
  108.0 0.0 copy-start
  108.0 0.8 copy.25
  108.8 0.4 copy-done
  109.2 0.0 copy-start.2
  109.2 0.8 copy.26
  110.0 0.1 copy-done.2
  110.1 0.6 copy.27
Async XLA Ops:
  106.1 1.9 %copy-start.1 = (bf16[2,128,1024]{2,1,0:T(8,128)(2,1)S(1)}, bf16[2,128,1024]{2,1,0:T(8,128)(2,1)}, u32[]{:S(2)}) copy-start(bf16[2,128,1024]{2,1,0:T(8,128)(2,1)} %get-tuple-element.22) | copy-start | bytes 1572868
  108.0 1.2 %copy-start = (bf16[2,128,1024]{2,1,0:T(8,128)(2,1)S(1)}, bf16[2,128,1024]{2,1,0:T(8,128)(2,1)}, u32[]{:S(2)}) copy-start(bf16[2,128,1024]{2,1,0:T(8,128)(2,1)} %get-tuple-element.23) | copy-start | bytes 1572868
  109.2 0.9 copy-start.2

commit v2 on v1

v2 whole, which is shorter than its diff:
```python
import jax
import jax.numpy as jnp
from jax import lax
from jax.experimental import pallas as pl
from jax.experimental.pallas import tpu as pltpu
from jax.sharding import PartitionSpec as P

MESH = pl.DeviceIdType.MESH
F32 = jnp.float32
BF16 = jnp.bfloat16
M, R, D, H, W = 2, 128, 1024, 32, 192
PAIRS = 8
CH = 13
MEMBERS = 16
CHANNELS = 100
SMOOTH = 0.1
NT = (((1,), (1,)), ((), ()))
TN = (((0,), (0,)), ((), ()))


def dot(a, b, dims=(((1,), (0,)), ((), ()))):
    return lax.dot_general(a, b, dims, preferred_element_type=F32)


def iota(shape, dim):
    return lax.broadcasted_iota(jnp.int32, shape, dim)


def kernel(
    L, Q, K, wsh, dec_h, tgt_h, srows_h, nbr_h, live_h, mult_h,
    o_loss, o_dl, o_dq, o_dk, o_dw,
    dec, tgt, srows, nbr, live, mult, qv,
    wg, wf, wl, kw, qt, lt, wlt, lk, oneh, snd_l, snd_k,
    decp, decpt, tgo, pf, pb, vv, outt, fs, fa, slf, terms, sl, sr, dot_t, dv, dk, rv, rk,
    e1s, e1r, s1, r1, a2, s2, r2, a3, s3, r3, s4, r4, fin, lsend, lrecv, gl, gq, gk, gw,
    ssem, rsem, lsem,
):
    e = lax.axis_index("ens")
    s = lax.axis_index("space")
    zh, c = e // 2, e % 2
    zl, y, x = s // 16, (s // 4) % 4, s % 4
    a = y * (1 - c) + x * c
    b = x * (1 - c) + y * c
    b_other = y * (1 - c) + x * c

    def at(e_, zl_, y_, x_):
        return (e_, zl_ * 16 + y_ * 4 + x_)

    sibling = (zh * 2 + 1 - c, s)

    def peer_a(k):
        return at(e, zl, (y + k * (1 - c)) % 4, (x + k * c) % 4)

    def peer_b(k):
        return at(e, zl, (y + k * c) % 4, (x + k * (1 - c)) % 4)

    def peer_zl(k):
        return at(e, (zl + k) % 4, y, x)

    def peer_zh(k):
        return (((zh + k) % 4) * 2 + c, s)

    def peer_ens(k):
        return ((e + k) % 8, s)

    right = (e, (s + 1) % 64)
    left = (e, (s + 63) % 64)

    barrier = pltpu.get_barrier_semaphore()
    partners = [peer_a(k) for k in (1, 2, 3)] + [peer_b(k) for k in (1, 2, 3)]
    partners += [peer_zl(k) for k in (1, 2, 3)] + [peer_ens(k) for k in range(1, 8)]
    partners += [right, left]
    for p in partners:
        pl.semaphore_signal(barrier, inc=1, device_id=p, device_id_type=MESH)

    sent = []
    count = [0]

    def send(src, dst, device):
        k = count[0]
        count[0] += 1
        copy = pltpu.make_async_remote_copy(
            src_ref=src, dst_ref=dst, send_sem=ssem.at[k], recv_sem=rsem.at[k],
            device_id=device, device_id_type=MESH,
        )
        copy.start()
        sent.append(copy)
        return copy

    fetched = []

    def fetch(src, dst):
        copy = pltpu.make_async_copy(src, dst, lsem.at[len(fetched)])
        fetched.append(copy)
        copy.start()
        return copy

    get_rows = fetch(srows_h, srows)
    get_k = fetch(K, kw.at[:, pl.ds(0, R)])
    get_l = fetch(L, wl.at[:, pl.ds(0, R)])
    own_half = pl.ds(pl.multiple_of(c * 512, 512), 512)
    get_w = fetch(wsh.at[:, own_half], wg.at[c, b, zl, a])
    get_q = fetch(Q, qv)
    get_small = [
        fetch(nbr_h, nbr), fetch(live_h, live), fetch(dec_h, dec), fetch(tgt_h, tgt), fetch(mult_h, mult)
    ]

    get_rows.wait()
    rows = iota((R, H), 0)
    to_right = (rows == srows[1:2, :]).astype(F32).astype(BF16)
    to_left = (rows == srows[0:1, :]).astype(F32).astype(BF16)
    oneh[:, 0:H] = to_right
    oneh[:, H:2 * H] = to_left
    get_k.wait()
    for m in range(M):
        snd_k[0, m] = dot(to_right, kw[m, 0:R], TN).astype(BF16)
        snd_k[1, m] = dot(to_left, kw[m, 0:R], TN).astype(BF16)
    get_l.wait()
    for m in range(M):
        snd_l[0, m] = dot(to_right, wl[m, 0:R], TN).astype(BF16)
        snd_l[1, m] = dot(to_left, wl[m, 0:R], TN).astype(BF16)
    get_w.wait()

    pl.semaphore_wait(barrier, len(partners))

    w1 = [send(wg.at[c, b, zl, a], wg.at[c, b, zl, a], peer_zl(k)) for k in (1, 2, 3)]
    hk = [
        send(snd_k.at[0], kw.at[:, pl.ds(R, H)], right),
        send(snd_k.at[1], kw.at[:, pl.ds(R + H, H)], left),
    ]

    def halo_latents():
        return [
            send(snd_l.at[0], wl.at[:, pl.ds(R, H)], right),
            send(snd_l.at[1], wl.at[:, pl.ds(R + H, H)], left),
        ]

    if HALO_AT == 0:
        hl = halo_latents()

    for copy in get_small:
        copy.wait()
    node_ids = nbr[...]
    row = iota((W, R), 0)
    wide_id = jnp.where(row < R, row + H, jnp.where(row < R + H, row - R, row))
    used = live[...]
    links = jnp.zeros((W, R), F32)
    for t in range(16):
        hit = jnp.where(used > t, node_ids[t:t + 1, :], -1) == wide_id
        links = links + jnp.where(hit, 1.0, 0.0)
    lk[:, 0:R] = links
    lk[:, R:2 * R] = links

    for k in range(3):
        w1[k].wait_recv()
    w2 = [send(wg.at[c, b, :, a], wg.at[c, b, :, a], peer_a(k)) for k in (1, 2, 3)]
    if HALO_AT == 2:
        hl = halo_latents()

    get_q.wait()
    for m in range(M):
        for d in range(8):
            qt[m, d * 128:(d + 1) * 128, :] = qv[m, :, d * 128:(d + 1) * 128].T
            lt[m, d * 128:(d + 1) * 128, :] = wl[m, 0:R, d * 128:(d + 1) * 128].T
    slot, chan = iota((128, CHANNELS), 0), iota((128, CHANNELS), 1)
    place = ((slot % 16 < CH) & (chan == (slot // 16) * CH + slot % 16)).astype(F32).astype(BF16)
    slot_t, chan_t = iota((CHANNELS, 128), 1), iota((CHANNELS, 128), 0)
    place_t = ((slot_t % 16 < CH) & (chan_t == (slot_t // 16) * CH + slot_t % 16)).astype(F32).astype(BF16)
    decp[...] = dot(dec[...], place_t, TN).astype(BF16)
    decpt[...] = dot(place, dec[...]).astype(BF16)
    slot16, chan16 = iota((16, CHANNELS), 0), iota((16, CHANNELS), 1)
    own_place = ((slot16 < CH) & (chan16 == e * CH + slot16)).astype(F32)
    tgo[...] = lax.dot_general(
        own_place, tgt[...], (((1,), (0,)), ((), ())),
        precision=lax.Precision.HIGHEST, preferred_element_type=F32,
    )

    for k in range(3):
        w2[k].wait_recv()
    w3 = [send(wg.at[c, b], wg.at[c, b], peer_b(k)) for k in (1, 2, 3)]
    wd = [send(wg.at[c, b], wg.at[c, b], sibling)]
    if HALO_AT == 3:
        hl = halo_latents()

    for k in range(2):
        hk[k].wait_recv()

    top = iota((128, R), 0) < 64

    def spread(block):
        zero = jnp.zeros_like(block)
        return jnp.concatenate([jnp.where(top, block, zero), jnp.where(top, zero, block)], axis=1)

    def folded(block):
        return jnp.where(top, block[:, 0:R], block[:, R:2 * R])

    def cols(p):
        return pl.ds(pl.multiple_of(p * 128, 128), 128)

    def weights_of(p, _):
        link = lk[...]
        for m in range(M):
            scores = dot(kw[m, :, cols(p)], spread(qt[m, cols(p), :])) * 0.125
            masked = jnp.where(link > 0, scores, -1e30)
            raised = link * jnp.exp(masked - jnp.max(masked, axis=0, keepdims=True))
            weight = raised * (1.0 / jnp.sum(raised, axis=0, keepdims=True))
            pf[m, p] = weight
            pb[m, p] = weight.astype(BF16)
        return 0

    lax.fori_loop(0, 4, weights_of, 0)
    for k in range(3):
        w3[k].wait_recv()
        bk = (b + 3 - k) % 4
        wd.append(send(wg.at[c, bk], wg.at[c, bk], sibling))
    lax.fori_loop(4, PAIRS, weights_of, 0)
    for k in range(2):
        hl[k].wait_recv()
    for k in range(4):
        wd[k].wait_recv()

    for z_ in range(4):
        for y_ in range(4):
            for x_ in range(4):
                d = z_ * 256 + y_ * 64 + x_ * 16
                wf[d:d + 16, 0:512] = wg[0, x_, z_, y_]
                wf[d:d + 16, 512:1024] = wg[1, y_, z_, x_]

    def mix(m):
        def step(p, _):
            mixed = folded(dot(vv[m, :, cols(p)], pb[m, p], TN))
            outt[m, cols(p), :] = (lt[m, cols(p), :].astype(F32) + mixed).astype(BF16)
            return 0
        return step

    def values_of(m):
        def step(q, _):
            block = pl.ds(pl.multiple_of(q * 256, 256), 256)
            vv[m, :, block] = dot(wl[m], wf[:, block]).astype(BF16)
            return 0
        return step

    fx = []
    for m in range(M):
        lax.fori_loop(0, 4, values_of(m), 0)
        lax.fori_loop(0, PAIRS, mix(m), 0)
        fs[m] = dot(decpt[...], outt[m]).reshape(8, 16, R)
        fa[2 * e + m] = fs[m, e]
        for k in range(1, 8):
            fx.append(send(fs.at[m, (e + k) % 8], fa.at[2 * e + m], peer_ens(k)))

    for m in range(M):
        for d in range(8):
            halo_t = wl[m, R:W, d * 128:(d + 1) * 128].T
            own_t = lt[m, d * 128:(d + 1) * 128, :]
            for i in range(8):
                g = d * 8 + i
                z_, y_, x_ = g // 16, (g // 4) % 4, g % 4
                r0 = (x_ * 16 + z_ * 4 + y_) * 16
                r1_ = (y_ * 16 + z_ * 4 + x_) * 16
                for h, r_ in ((0, r0), (1, r1_)):
                    wlt[h, m, r_:r_ + 16, 0:R] = own_t[i * 16:(i + 1) * 16]
                    wlt[h, m, r_:r_ + 16, R:W] = halo_t[i * 16:(i + 1) * 16]

    for copy in fx:
        copy.wait_recv()

    pair_norm = 1.0 / (MEMBERS * (MEMBERS - 1))

    def score(g, _):
        part = pl.ds(pl.multiple_of(g * 8, 8), 8)
        f = fa[:, part]
        shift = f - tgo[part][None]
        square = shift * shift + SMOOTH * SMOOTH
        inverse = lax.rsqrt(square)
        near = jnp.sum(square * inverse - SMOOTH, axis=0)
        pair_slope = jnp.zeros((MEMBERS, 8, R), F32)
        pair_total = jnp.zeros((8, R), F32)
        for k in range(1, 9):
            gap = f - jnp.concatenate([f[k:], f[:k]], axis=0)
            gap_square = gap * gap + SMOOTH * SMOOTH
            gap_inverse = lax.rsqrt(gap_square)
            radius = gap_square * gap_inverse - SMOOTH
            slope = gap * gap_inverse
            if k < 8:
                pair_total = pair_total + jnp.sum(radius, axis=0)
                back = jnp.concatenate([slope[MEMBERS - k:], slope[:MEMBERS - k]], axis=0)
                pair_slope = pair_slope + slope - back
            else:
                pair_total = pair_total + jnp.sum(radius[:8], axis=0)
                pair_slope = pair_slope + slope
        slf[:, part] = mult[0] * (shift * inverse * (1.0 / MEMBERS) - pair_slope * pair_norm)
        slot_id = iota((8, R), 0) + g * 8
        real = (slot_id < CH) & (slot_id + e * CH < CHANNELS)
        terms[g] = jnp.where(real, near * (1.0 / MEMBERS) - pair_total * pair_norm, 0.0)
        return 0

    lax.fori_loop(0, 2, score, 0)
    sl[...] = slf[...].astype(BF16)
    sx = [
        send(sl.at[pl.ds(2 * ((e + k) % 8), 2)], sr.at[e], peer_ens(k))
        for k in range(1, 8)
    ]
    sr[e] = sl[pl.ds(2 * e, 2)]
    lsend[0] = jnp.sum(terms[0] + terms[1], axis=0, keepdims=True)
    lrecv[0, zh] = lsend[0]
    l0 = [send(lsend.at[0], lrecv.at[0, zh], peer_zh(k)) for k in (1, 2, 3)]
    for copy in sx:
        copy.wait_recv()

    for m in range(M):
        dot_t[m] = dot(decp[...], sr[:, m].reshape(128, R)).astype(BF16)

    def value_grads(half, q):
        for i in range(2):
            p = half * 4 + q * 2 + i
            for m in range(M):
                dv[half, m, :, (q * 2 + i) * 128:(q * 2 + i + 1) * 128] = dot(
                    pb[m, p], spread(dot_t[m, cols(p), :]), NT
                ).astype(BF16)

    def weight_grad(half, q, block):
        block_rows = pl.ds(pl.multiple_of(block * 256, 256), 256)
        return dot(wlt[half, 0, block_rows, :], dv[half, 0, :, q * 256:(q + 1) * 256]) + dot(
            wlt[half, 1, block_rows, :], dv[half, 1, :, q * 256:(q + 1) * 256])

    def loss_step(stage, copies, mine, peers):
        for copy in copies:
            copy.wait_recv()
        got = lrecv[stage]
        if stage == 1:
            lsend[2] = got[0] + got[1]
        else:
            lsend[stage + 1] = (got[0] + got[1]) + (got[2] + got[3])
        lrecv[stage + 1, mine] = lsend[stage + 1]
        return [send(lsend.at[stage + 1], lrecv.at[stage + 1, mine], p) for p in peers]

    x1, x2, x3, x4, x5, x6 = ([None, None] for _ in range(6))
    for q in range(2):
        value_grads(1 - c, q)
        x1[q] = []
        for k in (1, 2, 3, 0):
            e1s[q, k] = weight_grad(1 - c, q, (b_other + k) % 4).astype(BF16)
            x1[q].append(send(e1s.at[q, k], e1r.at[q, k], sibling))
        value_grads(c, q)
        if q == 0:
            l1 = loss_step(0, l0, c, [sibling])
        else:
            hv = [
                send(dv.at[:, :, pl.ds(R + H, H)], rv.at[:, :, pl.ds(H, H)], right),
                send(dv.at[:, :, pl.ds(R, H)], rv.at[:, :, pl.ds(0, H)], left),
            ]
        x2[q] = []
        for i, k in enumerate((1, 2, 3, 0)):
            total = weight_grad(c, q, (b + k) % 4)
            x1[q][i].wait_recv()
            total = total + e1r[q, k].astype(F32)
            if k:
                s1[q, k - 1] = total.astype(BF16)
                x2[q].append(send(s1.at[q, k - 1], r1.at[q, k - 1], peer_b(k)))
            else:
                a2[q] = total.reshape(4, 4, 16, 256)

    def attention_grads(p, _):
        for m in range(M):
            grad_weight = dot(vv[m, :, cols(p)], spread(dot_t[m, cols(p), :])).astype(BF16).astype(F32)
            weight = pf[m, p]
            drift = jnp.sum(grad_weight * weight, axis=0, keepdims=True)
            grad_scores = (weight * (grad_weight - drift) * 0.125).astype(BF16)
            dk[m, :, cols(p)] = dot(grad_scores, spread(qt[m, cols(p), :]), NT).astype(BF16)
            grad_q = folded(dot(kw[m, :, cols(p)], grad_scores, TN))
            gq[m, :, cols(p)] = grad_q.astype(BF16).T
        return 0

    def second(q):
        for copy in x2[q]:
            copy.wait_recv()
        a2[q] = a2[q] + (
            r1[q, 0].astype(F32) + r1[q, 1].astype(F32) + r1[q, 2].astype(F32)
        ).reshape(4, 4, 16, 256)
        x3[q] = []
        for k in (1, 2, 3):
            s2[q, k - 1] = a2[q, :, (a + k) % 4].astype(BF16)
            x3[q].append(send(s2.at[q, k - 1], r2.at[q, k - 1], peer_a(k)))

    def third(q):
        for copy in x3[q]:
            copy.wait_recv()
        a3[q] = a2[q, :, a] + (r2[q, 0].astype(F32) + r2[q, 1].astype(F32) + r2[q, 2].astype(F32))
        x4[q] = []
        for k in (1, 2, 3):
            s3[q, k - 1] = a3[q, (zl + k) % 4].astype(BF16)
            x4[q].append(send(s3.at[q, k - 1], r3.at[q, k - 1], peer_zl(k)))

    def fourth(q):
        for copy in x4[q]:
            copy.wait_recv()
        s4[q] = (
            a3[q, zl] + (r3[q, 0].astype(F32) + r3[q, 1].astype(F32) + r3[q, 2].astype(F32))
        ).astype(BF16)
        r4[q, zh] = s4[q]
        x5[q] = [send(s4.at[q], r4.at[q, zh], peer_zh(k)) for k in (1, 2, 3)]

    def fifth(q):
        for copy in x5[q]:
            copy.wait_recv()
        fin[c, q] = (r4[q, 0].astype(F32) + r4[q, 1].astype(F32)) + (
            r4[q, 2].astype(F32) + r4[q, 3].astype(F32))
        x6[q] = send(fin.at[c, q], fin.at[c, q], sibling)

    def latent_grads(m):
        parts = [
            (dv[h, m, 0:R].astype(F32) + dot(oneh[...], rv[h, m])).astype(BF16) for h in range(2)
        ]
        out = dot(sr[:, m].reshape(128, R), decpt[...], TN).astype(BF16).astype(F32)
        out = out + dot(parts[0], wf[:, 0:512], NT) + dot(parts[1], wf[:, 512:1024], NT)
        gl[m] = out.astype(BF16)

    lax.fori_loop(0, 2, attention_grads, 0)
    l2 = loss_step(1, l1, b, [peer_b(k) for k in (1, 2, 3)])
    second(0)
    lax.fori_loop(2, 4, attention_grads, 0)
    second(1)
    lax.fori_loop(4, 6, attention_grads, 0)
    l3 = loss_step(2, l2, a, [peer_a(k) for k in (1, 2, 3)])
    third(0)
    lax.fori_loop(6, PAIRS, attention_grads, 0)
    third(1)
    hkb = [
        send(dk.at[:, pl.ds(R + H, H)], rk.at[:, pl.ds(H, H)], right),
        send(dk.at[:, pl.ds(R, H)], rk.at[:, pl.ds(0, H)], left),
    ]
    store = [fetch(gq, o_dq)]
    l4 = loss_step(3, l3, zl, [peer_zl(k) for k in (1, 2, 3)])
    for copy in hv:
        copy.wait_recv()
    fourth(0)
    latent_grads(0)
    fourth(1)
    latent_grads(1)
    store.append(fetch(gl, o_dl))
    l5 = loss_step(4, l4, c, [sibling])
    for copy in hkb:
        copy.wait_recv()
    for m in range(M):
        gk[m] = (dk[m, 0:R].astype(F32) + dot(oneh[...], rk[m])).astype(BF16)
    store.append(fetch(gk, o_dk))
    fifth(0)
    fifth(1)
    l5[0].wait_recv()
    o_loss[0, 0] = jnp.sum(lrecv[5, 0]) * (1.0 / (8192 * CHANNELS))
    for q in range(2):
        x6[q].wait_recv()
        for h in range(2):
            gw[:, h * 512 + q * 256:h * 512 + (q + 1) * 256] = fin[h, q]
    store.append(fetch(gw, o_dw))
    for copy in sent:
        copy.wait_send()
    for copy in store:
        copy.wait()


def hand_over(*refs):
    sources, results, held, sems = refs[:4], refs[4:8], refs[8:12], refs[12]
    arriving = [pltpu.make_async_copy(sources[i], held[i], sems.at[0, i]) for i in range(4)]
    leaving = [pltpu.make_async_copy(held[i], results[i], sems.at[1, i]) for i in range(4)]
    for copy in arriving:
        copy.start()
    for i in range(4):
        arriving[i].wait()
        leaving[i].start()
    for copy in leaving:
        copy.wait()


HALO_AT = 2
N_COPIES = 112


def body(latents, queries, attn_keys, value_weight, decoder, targets, send_rows, neighbours, live_slots, loss_multiplier):
    hbm = pl.BlockSpec(memory_space=pl.ANY)
    sm = pl.BlockSpec(memory_space=pltpu.SMEM)

    def buf(*shape, dtype=BF16):
        return pltpu.VMEM(shape, dtype)

    scratch = [
        buf(CHANNELS, D),
        buf(CHANNELS, R, dtype=F32),
        buf(2, H, dtype=jnp.int32),
        buf(16, R, dtype=jnp.int32),
        buf(1, R, dtype=jnp.int32),
        pltpu.SMEM((1,), F32),
        buf(M, R, D),
        buf(2, 4, 4, 4, 16, 512),
        buf(D, D),
        buf(M, W, D),
        buf(M, W, D),
        buf(M, D, R),
        buf(M, D, R),
        buf(2, M, D, W),
        buf(W, 2 * R, dtype=F32),
        buf(R, 2 * H),
        buf(2, M, H, D),
        buf(2, M, H, D),
        buf(D, 128),
        buf(128, D),
        buf(16, R, dtype=F32),
        buf(M, PAIRS, W, 2 * R, dtype=F32),
        buf(M, PAIRS, W, 2 * R),
        buf(M, W, D),
        buf(M, D, R),
        buf(M, 8, 16, R, dtype=F32),
        buf(MEMBERS, 16, R, dtype=F32),
        buf(MEMBERS, 16, R, dtype=F32),
        buf(2, 8, R, dtype=F32),
        buf(MEMBERS, 16, R),
        buf(8, M, 16, R),
        buf(M, D, R),
        buf(2, M, W, 512),
        buf(M, W, D),
        buf(2, M, 2 * H, 512),
        buf(M, 2 * H, D),
        buf(2, 4, 256, 256),
        buf(2, 4, 256, 256),
        buf(2, 3, 256, 256),
        buf(2, 3, 256, 256),
        buf(2, 4, 4, 16, 256, dtype=F32),
        buf(2, 3, 4, 16, 256),
        buf(2, 3, 4, 16, 256),
        buf(2, 4, 16, 256, dtype=F32),
        buf(2, 3, 16, 256),
        buf(2, 3, 16, 256),
        buf(2, 16, 256),
        buf(2, 4, 16, 256),
        buf(2, 2, 16, 256, dtype=F32),
        buf(6, 1, 128, dtype=F32),
        buf(6, 4, 1, 128, dtype=F32),
        buf(M, R, D),
        buf(M, R, D),
        buf(M, R, D),
        buf(16, D, dtype=F32),
        pltpu.SemaphoreType.DMA((N_COPIES,)),
        pltpu.SemaphoreType.DMA((N_COPIES,)),
        pltpu.SemaphoreType.DMA((16,)),
    ]
    loss, dl, dq, dk, dw = pl.pallas_call(
        kernel,
        out_shape=(
            jax.ShapeDtypeStruct((1, 1), F32),
            jax.ShapeDtypeStruct((M, R, D), BF16),
            jax.ShapeDtypeStruct((M, R, D), BF16),
            jax.ShapeDtypeStruct((M, R, D), BF16),
            jax.ShapeDtypeStruct((16, D), F32),
        ),
        in_specs=[hbm] * 10,
        out_specs=(sm, hbm, hbm, hbm, hbm),
        scratch_shapes=scratch,
        compiler_params=pltpu.CompilerParams(
            collective_id=0, has_side_effects=True, vmem_limit_bytes=56 * 1024 * 1024
        ),
    )(
        latents, queries, attn_keys, value_weight, decoder.T, targets, send_rows, neighbours.T,
        live_slots.reshape(1, R), loss_multiplier,
    )
    results = (dl, dq, dk, dw)
    dl, dq, dk, dw = pl.pallas_call(
        hand_over,
        out_shape=tuple(jax.ShapeDtypeStruct(r.shape, r.dtype) for r in results),
        in_specs=[hbm] * 4,
        out_specs=(hbm,) * 4,
        scratch_shapes=[pltpu.VMEM(r.shape, r.dtype) for r in results] + [pltpu.SemaphoreType.DMA((2, 4))],
    )(*results)
    return loss.reshape(1), dl, dq, dk, dw


def solution(mesh):
    rows = P("ens", "space", None)
    in_specs = (
        rows, rows, rows, P("space", None), P(), P(None, "space"), P(None, "space"),
        P("space", None), P("space"), P(),
    )
    out_specs = (P(), rows, rows, rows, P("space", None))
    return jax.shard_map(body, mesh=mesh, in_specs=in_specs, out_specs=out_specs, check_vma=False)
```

time: 112 us -> 105 us (0.938)
  local copies, waits for them, and re-layouts: 7.87 us -> 0 us
    unnamed x12 -> x0, local copies, waits for them, and re-layouts: 7.87 us -> none
    pallas_call x0 -> x1, Pallas kernels: none -> 2.26 us  [body(): pl.pallas_call(hand_over, out_shape=tuple((jax.ShapeDtypeStruct(r.shape,...]
    pallas_call x1, Pallas kernels: 101 us -> 99.5 us  [body(): pl.pallas_call(kernel, out_shape=(jax.ShapeDtypeStruct((1, 1), F32), jax....]
where the time goes in v2:
time: 105 us
  Pallas kernels  102 us (97%)
  between operations  3.04 us (3%)
    pallas_call x1, Pallas kernels, body(): pl.pallas_call(kernel, out_shape=(jax.ShapeDtypeStruct((1, 1), F32), jax....  99.5 us
    pallas_call x1, Pallas kernels, body(): pl.pallas_call(hand_over, out_shape=tuple((jax.ShapeDtypeStruct(r.shape,...  2.26 us

profile of v2, /device:TPU:1, one launch (start us, length us, event | category | flops | bytes accessed | tf_op | source)
XLA Modules:
  0.0 104.8 jit_solution(957378695158283676)
XLA Ops:
  1.3 99.5 %shard_map.137 = (f32[1,1]{1,0:T(1,128)}, bf16[2,128,1024]{2,1,0:T(8,128)(2,1)}, bf16[2,128,1024]{2,1,0:T(8,128)(2,1)}, bf16[2,128,1024]{2,1,0:T(8,128)(2,1)}, f32[16,1024]{1,0:T(8,128)}) custom-call(bf16[2,128,1024]{2,1,0:T(8,128)(2,1)} %L.1, bf16[2,128,1024]{2,1,0:T(8,128)(2,1)} %Q.1, bf16[2,128,1024]{2,1,0:T(8,128)(2,1)} %K.1, bf16[16,1024]{1,0:T(8,128)(2,1)} %wsh.1, ...), custom_call_target="tpu_custom_call" | custom-call | tf_op jit(solution)/shard_map/pallas_call | solution.py:547
  100.8 2.3 %shard_map.138 = (bf16[2,128,1024]{2,1,0:T(8,128)(2,1)}, bf16[2,128,1024]{2,1,0:T(8,128)(2,1)}, bf16[2,128,1024]{2,1,0:T(8,128)(2,1)}, f32[16,1024]{1,0:T(8,128)}) custom-call(bf16[2,128,1024]{2,1,0:T(8,128)(2,1)} %get-tuple-element.15.refs_0_, bf16[2,128,1024]{2,1,0:T(8,128)(2,1)} %get-tuple-element.16.refs_1_, ...), custom_call_target="tpu_custom_call" | custom-call | tf_op jit(solution)/shard_map/pallas_call | solution.py:567

commit v3 on v2

--- a/solution.py
+++ b/solution.py
@@ -124,19 +124,19 @@
     pl.semaphore_wait(barrier, len(partners))
 
     w1 = [send(wg.at[c, b, zl, a], wg.at[c, b, zl, a], peer_zl(k)) for k in (1, 2, 3)]
-    hk = [
-        send(snd_k.at[0], kw.at[:, pl.ds(R, H)], right),
-        send(snd_k.at[1], kw.at[:, pl.ds(R + H, H)], left),
-    ]
+    def halo_keys():
+        return [
+            send(snd_k.at[0], kw.at[:, pl.ds(R, H)], right),
+            send(snd_k.at[1], kw.at[:, pl.ds(R + H, H)], left),
+        ]
+
+    hk = halo_keys()
 
     def halo_latents():
         return [
             send(snd_l.at[0], wl.at[:, pl.ds(R, H)], right),
             send(snd_l.at[1], wl.at[:, pl.ds(R + H, H)], left),
         ]
-
-    if HALO_AT == 0:
-        hl = halo_latents()
 
     for copy in get_small:
         copy.wait()
@@ -154,8 +154,7 @@
     for k in range(3):
         w1[k].wait_recv()
     w2 = [send(wg.at[c, b, :, a], wg.at[c, b, :, a], peer_a(k)) for k in (1, 2, 3)]
-    if HALO_AT == 2:
-        hl = halo_latents()
+    hl = halo_latents()
 
     get_q.wait()
     for m in range(M):
@@ -179,8 +178,6 @@
         w2[k].wait_recv()
     w3 = [send(wg.at[c, b], wg.at[c, b], peer_b(k)) for k in (1, 2, 3)]
     wd = [send(wg.at[c, b], wg.at[c, b], sibling)]
-    if HALO_AT == 3:
-        hl = halo_latents()
 
     for k in range(2):
         hk[k].wait_recv()
@@ -208,12 +205,12 @@
             pb[m, p] = weight.astype(BF16)
         return 0
 
-    lax.fori_loop(0, 4, weights_of, 0)
+    lax.fori_loop(0, 4, weights_of, 0, unroll=2)
     for k in range(3):
         w3[k].wait_recv()
         bk = (b + 3 - k) % 4
         wd.append(send(wg.at[c, bk], wg.at[c, bk], sibling))
-    lax.fori_loop(4, PAIRS, weights_of, 0)
+    lax.fori_loop(4, PAIRS, weights_of, 0, unroll=2)
     for k in range(2):
         hl[k].wait_recv()
     for k in range(4):
@@ -233,17 +230,17 @@
             return 0
         return step
 
-    def values_of(m):
-        def step(q, _):
-            block = pl.ds(pl.multiple_of(q * 256, 256), 256)
-            vv[m, :, block] = dot(wl[m], wf[:, block]).astype(BF16)
-            return 0
-        return step
-
+    def values_of(q, _):
+        block = pl.ds(pl.multiple_of(q * 256, 256), 256)
+        both = dot(wl[...].reshape(M * W, D), wf[:, block]).astype(BF16)
+        for m in range(M):
+            vv[m, :, block] = both[m * W:(m + 1) * W]
+        return 0
+
+    lax.fori_loop(0, 4, values_of, 0)
     fx = []
     for m in range(M):
-        lax.fori_loop(0, 4, values_of(m), 0)
-        lax.fori_loop(0, PAIRS, mix(m), 0)
+        lax.fori_loop(0, PAIRS, mix(m), 0, unroll=4)
         fs[m] = dot(decpt[...], outt[m]).reshape(8, 16, R)
         fa[2 * e + m] = fs[m, e]
         for k in range(1, 8):
@@ -343,13 +340,6 @@
             e1s[q, k] = weight_grad(1 - c, q, (b_other + k) % 4).astype(BF16)
             x1[q].append(send(e1s.at[q, k], e1r.at[q, k], sibling))
         value_grads(c, q)
-        if q == 0:
-            l1 = loss_step(0, l0, c, [sibling])
-        else:
-            hv = [
-                send(dv.at[:, :, pl.ds(R + H, H)], rv.at[:, :, pl.ds(H, H)], right),
-                send(dv.at[:, :, pl.ds(R, H)], rv.at[:, :, pl.ds(0, H)], left),
-            ]
         x2[q] = []
         for i, k in enumerate((1, 2, 3, 0)):
             total = weight_grad(c, q, (b + k) % 4)
@@ -361,6 +351,12 @@
             else:
                 a2[q] = total.reshape(4, 4, 16, 256)
 
+    hv = [
+        send(dv.at[:, :, pl.ds(R + H, H)], rv.at[:, :, pl.ds(H, H)], right),
+        send(dv.at[:, :, pl.ds(R, H)], rv.at[:, :, pl.ds(0, H)], left),
+    ]
+    l1 = loss_step(0, l0, c, [sibling])
+
     def attention_grads(p, _):
         for m in range(M):
             grad_weight = dot(vv[m, :, cols(p)], spread(dot_t[m, cols(p), :])).astype(BF16).astype(F32)
@@ -416,15 +412,15 @@
         out = out + dot(parts[0], wf[:, 0:512], NT) + dot(parts[1], wf[:, 512:1024], NT)
         gl[m] = out.astype(BF16)
 
-    lax.fori_loop(0, 2, attention_grads, 0)
+    lax.fori_loop(0, 2, attention_grads, 0, unroll=2)
     l2 = loss_step(1, l1, b, [peer_b(k) for k in (1, 2, 3)])
     second(0)
-    lax.fori_loop(2, 4, attention_grads, 0)
+    lax.fori_loop(2, 4, attention_grads, 0, unroll=2)
     second(1)
-    lax.fori_loop(4, 6, attention_grads, 0)
+    lax.fori_loop(4, 6, attention_grads, 0, unroll=2)
     l3 = loss_step(2, l2, a, [peer_a(k) for k in (1, 2, 3)])
     third(0)
-    lax.fori_loop(6, PAIRS, attention_grads, 0)
+    lax.fori_loop(6, PAIRS, attention_grads, 0, unroll=2)
     third(1)
     hkb = [
         send(dk.at[:, pl.ds(R + H, H)], rk.at[:, pl.ds(H, H)], right),
@@ -432,11 +428,11 @@
     ]
     store = [fetch(gq, o_dq)]
     l4 = loss_step(3, l3, zl, [peer_zl(k) for k in (1, 2, 3)])
+    fourth(0)
+    fourth(1)
     for copy in hv:
         copy.wait_recv()
-    fourth(0)
     latent_grads(0)
-    fourth(1)
     latent_grads(1)
     store.append(fetch(gl, o_dl))
     l5 = loss_step(4, l4, c, [sibling])
@@ -473,7 +469,6 @@
         copy.wait()
 
 
-HALO_AT = 2
 N_COPIES = 112
 
 

time: 105 us -> 99.7 us (0.950)
  Pallas kernels: 102 us -> 96.5 us
    pallas_call x1, Pallas kernels: 99.5 us -> 94.2 us  [body(): pl.pallas_call(kernel, out_shape=(jax.ShapeDtypeStruct((1, 1), F32), jax....]
where the time goes in v3:
time: 99.7 us; the launch traced here: 99.5 us
  Pallas kernels  96.5 us (97%)
  between operations  3.04 us (3%)
    pallas_call x1, Pallas kernels, body(): pl.pallas_call(kernel, out_shape=(jax.ShapeDtypeStruct((1, 1), F32), jax....  94.2 us
    pallas_call x1, Pallas kernels, body(): pl.pallas_call(hand_over, out_shape=tuple((jax.ShapeDtypeStruct(r.shape,...  2.26 us

profile of v3, /device:TPU:1, one launch (start us, length us, event | category | flops | bytes accessed | tf_op | source)
XLA Modules:
  0.0 99.5 jit_solution(11146304262207117986)
XLA Ops:
  1.3 94.2 %shard_map.137 = (f32[1,1]{1,0:T(1,128)}, bf16[2,128,1024]{2,1,0:T(8,128)(2,1)}, bf16[2,128,1024]{2,1,0:T(8,128)(2,1)}, bf16[2,128,1024]{2,1,0:T(8,128)(2,1)}, f32[16,1024]{1,0:T(8,128)}) custom-call(bf16[2,128,1024]{2,1,0:T(8,128)(2,1)} %L.1, bf16[2,128,1024]{2,1,0:T(8,128)(2,1)} %Q.1, bf16[2,128,1024]{2,1,0:T(8,128)(2,1)} %K.1, bf16[16,1024]{1,0:T(8,128)(2,1)} %wsh.1, ...), custom_call_target="tpu_custom_call" | custom-call | tf_op jit(solution)/shard_map/pallas_call | solution.py:542
  95.5 2.3 %shard_map.138 = (bf16[2,128,1024]{2,1,0:T(8,128)(2,1)}, bf16[2,128,1024]{2,1,0:T(8,128)(2,1)}, bf16[2,128,1024]{2,1,0:T(8,128)(2,1)}, f32[16,1024]{1,0:T(8,128)}) custom-call(bf16[2,128,1024]{2,1,0:T(8,128)(2,1)} %get-tuple-element.15.refs_0_, bf16[2,128,1024]{2,1,0:T(8,128)(2,1)} %get-tuple-element.16.refs_1_, ...), custom_call_target="tpu_custom_call" | custom-call | tf_op jit(solution)/shard_map/pallas_call | solution.py:562

commit v4 on v3

--- a/solution.py
+++ b/solution.py
@@ -105,6 +105,7 @@
         fetch(nbr_h, nbr), fetch(live_h, live), fetch(dec_h, dec), fetch(tgt_h, tgt), fetch(mult_h, mult)
     ]
 
+    fa[:, CH:16] = jnp.zeros((MEMBERS, 16 - CH, R), F32)
     get_rows.wait()
     rows = iota((R, H), 0)
     to_right = (rows == srows[1:2, :]).astype(F32).astype(BF16)
@@ -176,7 +177,11 @@
 
     for k in range(3):
         w2[k].wait_recv()
-    w3 = [send(wg.at[c, b], wg.at[c, b], peer_b(k)) for k in (1, 2, 3)]
+    parts = [pl.ds(0, 256), pl.ds(256, 256)]
+    w3 = [
+        [send(wg.at[c, b, :, :, :, part], wg.at[c, b, :, :, :, part], peer_b(k)) for k in (1, 3, 2)]
+        for part in parts
+    ]
     wd = [send(wg.at[c, b], wg.at[c, b], sibling)]
 
     for k in range(2):
@@ -206,15 +211,16 @@
         return 0
 
     lax.fori_loop(0, 4, weights_of, 0, unroll=2)
-    for k in range(3):
-        w3[k].wait_recv()
-        bk = (b + 3 - k) % 4
-        wd.append(send(wg.at[c, bk], wg.at[c, bk], sibling))
+    for h, part in enumerate(parts):
+        for i, k in enumerate((1, 3, 2)):
+            w3[h][i].wait_recv()
+            bk = (b + 4 - k) % 4
+            wd.append(send(wg.at[c, bk, :, :, :, part], wg.at[c, bk, :, :, :, part], sibling))
     lax.fori_loop(4, PAIRS, weights_of, 0, unroll=2)
     for k in range(2):
         hl[k].wait_recv()
-    for k in range(4):
-        wd[k].wait_recv()
+    for copy in wd:
+        copy.wait_recv()
 
     for z_ in range(4):
         for y_ in range(4):
@@ -244,7 +250,7 @@
         fs[m] = dot(decpt[...], outt[m]).reshape(8, 16, R)
         fa[2 * e + m] = fs[m, e]
         for k in range(1, 8):
-            fx.append(send(fs.at[m, (e + k) % 8], fa.at[2 * e + m], peer_ens(k)))
+            fx.append(send(fs.at[m, (e + k) % 8, pl.ds(0, CH)], fa.at[2 * e + m, pl.ds(0, CH)], peer_ens(k)))
 
     for m in range(M):
         for d in range(8):
@@ -351,10 +357,6 @@
             else:
                 a2[q] = total.reshape(4, 4, 16, 256)
 
-    hv = [
-        send(dv.at[:, :, pl.ds(R + H, H)], rv.at[:, :, pl.ds(H, H)], right),
-        send(dv.at[:, :, pl.ds(R, H)], rv.at[:, :, pl.ds(0, H)], left),
-    ]
     l1 = loss_step(0, l0, c, [sibling])
 
     def attention_grads(p, _):
@@ -417,6 +419,10 @@
     second(0)
     lax.fori_loop(2, 4, attention_grads, 0, unroll=2)
     second(1)
+    hv = [
+        send(dv.at[:, :, pl.ds(R + H, H)], rv.at[:, :, pl.ds(H, H)], right),
+        send(dv.at[:, :, pl.ds(R, H)], rv.at[:, :, pl.ds(0, H)], left),
+    ]
     lax.fori_loop(4, 6, attention_grads, 0, unroll=2)
     l3 = loss_step(2, l2, a, [peer_a(k) for k in (1, 2, 3)])
     third(0)

time: 99.7 us -> 99.5 us (level)
  no operation moved by 1% of the time
where the time goes in v4:
time: 99.5 us; the launch traced here: 99.3 us
  Pallas kernels  96.3 us (97%)
  between operations  3.04 us (3%)
    pallas_call x1, Pallas kernels, body(): pl.pallas_call(kernel, out_shape=(jax.ShapeDtypeStruct((1, 1), F32), jax....  94 us
    pallas_call x1, Pallas kernels, body(): pl.pallas_call(hand_over, out_shape=tuple((jax.ShapeDtypeStruct(r.shape,...  2.26 us

profile of v4, /device:TPU:1, one launch (start us, length us, event | category | flops | bytes accessed | tf_op | source)
XLA Modules:
  0.0 99.3 jit_solution(3134585966609010880)
XLA Ops:
  1.3 94.0 %shard_map.137 = (f32[1,1]{1,0:T(1,128)}, bf16[2,128,1024]{2,1,0:T(8,128)(2,1)}, bf16[2,128,1024]{2,1,0:T(8,128)(2,1)}, bf16[2,128,1024]{2,1,0:T(8,128)(2,1)}, f32[16,1024]{1,0:T(8,128)}) custom-call(bf16[2,128,1024]{2,1,0:T(8,128)(2,1)} %L.1, bf16[2,128,1024]{2,1,0:T(8,128)(2,1)} %Q.1, bf16[2,128,1024]{2,1,0:T(8,128)(2,1)} %K.1, bf16[16,1024]{1,0:T(8,128)(2,1)} %wsh.1, ...), custom_call_target="tpu_custom_call" | custom-call | tf_op jit(solution)/shard_map/pallas_call | solution.py:548
  95.3 2.3 %shard_map.138 = (bf16[2,128,1024]{2,1,0:T(8,128)(2,1)}, bf16[2,128,1024]{2,1,0:T(8,128)(2,1)}, bf16[2,128,1024]{2,1,0:T(8,128)(2,1)}, f32[16,1024]{1,0:T(8,128)}) custom-call(bf16[2,128,1024]{2,1,0:T(8,128)(2,1)} %get-tuple-element.15.refs_0_, bf16[2,128,1024]{2,1,0:T(8,128)(2,1)} %get-tuple-element.16.refs_1_, ...), custom_call_target="tpu_custom_call" | custom-call | tf_op jit(solution)/shard_map/pallas_call | solution.py:568

commit v5 on v4

--- a/solution.py
+++ b/solution.py
@@ -13,6 +13,7 @@
 CH = 13
 MEMBERS = 16
 CHANNELS = 100
+FAR_FIRST = (4, 3, 5, 2, 6, 1, 7)
 SMOOTH = 0.1
 NT = (((1,), (1,)), ((), ()))
 TN = (((0,), (0,)), ((), ()))
@@ -179,7 +180,7 @@
         w2[k].wait_recv()
     parts = [pl.ds(0, 256), pl.ds(256, 256)]
     w3 = [
-        [send(wg.at[c, b, :, :, :, part], wg.at[c, b, :, :, :, part], peer_b(k)) for k in (1, 3, 2)]
+        [send(wg.at[c, b, :, :, :, part], wg.at[c, b, :, :, :, part], peer_b(k)) for k in (2, 1, 3)]
         for part in parts
     ]
     wd = [send(wg.at[c, b], wg.at[c, b], sibling)]
@@ -212,7 +213,7 @@
 
     lax.fori_loop(0, 4, weights_of, 0, unroll=2)
     for h, part in enumerate(parts):
-        for i, k in enumerate((1, 3, 2)):
+        for i, k in enumerate((2, 1, 3)):
             w3[h][i].wait_recv()
             bk = (b + 4 - k) % 4
             wd.append(send(wg.at[c, bk, :, :, :, part], wg.at[c, bk, :, :, :, part], sibling))
@@ -249,7 +250,7 @@
         lax.fori_loop(0, PAIRS, mix(m), 0, unroll=4)
         fs[m] = dot(decpt[...], outt[m]).reshape(8, 16, R)
         fa[2 * e + m] = fs[m, e]
-        for k in range(1, 8):
+        for k in FAR_FIRST:
             fx.append(send(fs.at[m, (e + k) % 8, pl.ds(0, CH)], fa.at[2 * e + m, pl.ds(0, CH)], peer_ens(k)))
 
     for m in range(M):
@@ -302,12 +303,12 @@
     sl[...] = slf[...].astype(BF16)
     sx = [
         send(sl.at[pl.ds(2 * ((e + k) % 8), 2)], sr.at[e], peer_ens(k))
-        for k in range(1, 8)
+        for k in FAR_FIRST
     ]
     sr[e] = sl[pl.ds(2 * e, 2)]
     lsend[0] = jnp.sum(terms[0] + terms[1], axis=0, keepdims=True)
     lrecv[0, zh] = lsend[0]
-    l0 = [send(lsend.at[0], lrecv.at[0, zh], peer_zh(k)) for k in (1, 2, 3)]
+    l0 = [send(lsend.at[0], lrecv.at[0, zh], peer_zh(k)) for k in (2, 1, 3)]
     for copy in sx:
         copy.wait_recv()
 
@@ -342,12 +343,12 @@
     for q in range(2):
         value_grads(1 - c, q)
         x1[q] = []
-        for k in (1, 2, 3, 0):
+        for k in (2, 1, 3, 0):
             e1s[q, k] = weight_grad(1 - c, q, (b_other + k) % 4).astype(BF16)
             x1[q].append(send(e1s.at[q, k], e1r.at[q, k], sibling))
         value_grads(c, q)
         x2[q] = []
-        for i, k in enumerate((1, 2, 3, 0)):
+        for i, k in enumerate((2, 1, 3, 0)):
             total = weight_grad(c, q, (b + k) % 4)
             x1[q][i].wait_recv()
             total = total + e1r[q, k].astype(F32)
@@ -377,7 +378,7 @@
             r1[q, 0].astype(F32) + r1[q, 1].astype(F32) + r1[q, 2].astype(F32)
         ).reshape(4, 4, 16, 256)
         x3[q] = []
-        for k in (1, 2, 3):
+        for k in (2, 1, 3):
             s2[q, k - 1] = a2[q, :, (a + k) % 4].astype(BF16)
             x3[q].append(send(s2.at[q, k - 1], r2.at[q, k - 1], peer_a(k)))
 
@@ -397,7 +398,7 @@
             a3[q, zl] + (r3[q, 0].astype(F32) + r3[q, 1].astype(F32) + r3[q, 2].astype(F32))
         ).astype(BF16)
         r4[q, zh] = s4[q]
-        x5[q] = [send(s4.at[q], r4.at[q, zh], peer_zh(k)) for k in (1, 2, 3)]
+        x5[q] = [send(s4.at[q], r4.at[q, zh], peer_zh(k)) for k in (2, 1, 3)]
 
     def fifth(q):
         for copy in x5[q]:

time: 99.5 us -> 97.7 us (0.982)
  Pallas kernels: 96.3 us -> 94.4 us
    pallas_call x1, Pallas kernels: 94 us -> 92.2 us  [body(): pl.pallas_call(kernel, out_shape=(jax.ShapeDtypeStruct((1, 1), F32), jax....]
where the time goes in v5:
time: 97.7 us; the launch traced here: 97.5 us
  Pallas kernels  94.4 us (97%)
  between operations  3.04 us (3%)
    pallas_call x1, Pallas kernels, body(): pl.pallas_call(kernel, out_shape=(jax.ShapeDtypeStruct((1, 1), F32), jax....  92.2 us
    pallas_call x1, Pallas kernels, body(): pl.pallas_call(hand_over, out_shape=tuple((jax.ShapeDtypeStruct(r.shape,...  2.26 us

profile of v5, /device:TPU:1, one launch (start us, length us, event | category | flops | bytes accessed | tf_op | source)
XLA Modules:
  0.0 97.5 jit_solution(16869484628203532596)
XLA Ops:
  1.3 92.2 %shard_map.137 = (f32[1,1]{1,0:T(1,128)}, bf16[2,128,1024]{2,1,0:T(8,128)(2,1)}, bf16[2,128,1024]{2,1,0:T(8,128)(2,1)}, bf16[2,128,1024]{2,1,0:T(8,128)(2,1)}, f32[16,1024]{1,0:T(8,128)}) custom-call(bf16[2,128,1024]{2,1,0:T(8,128)(2,1)} %L.1, bf16[2,128,1024]{2,1,0:T(8,128)(2,1)} %Q.1, bf16[2,128,1024]{2,1,0:T(8,128)(2,1)} %K.1, bf16[16,1024]{1,0:T(8,128)(2,1)} %wsh.1, ...), custom_call_target="tpu_custom_call" | custom-call | tf_op jit(solution)/shard_map/pallas_call | solution.py:549
  93.5 2.3 %shard_map.138 = (bf16[2,128,1024]{2,1,0:T(8,128)(2,1)}, bf16[2,128,1024]{2,1,0:T(8,128)(2,1)}, bf16[2,128,1024]{2,1,0:T(8,128)(2,1)}, f32[16,1024]{1,0:T(8,128)}) custom-call(bf16[2,128,1024]{2,1,0:T(8,128)(2,1)} %get-tuple-element.15.refs_0_, bf16[2,128,1024]{2,1,0:T(8,128)(2,1)} %get-tuple-element.16.refs_1_, ...), custom_call_target="tpu_custom_call" | custom-call | tf_op jit(solution)/shard_map/pallas_call | solution.py:569
